TPU v7x, 128 devices: a whole 4x4x4 slice. The times are simulated.
128 devices in a mesh: pair: 32 (over z_hi, y, x), ao: 4 (over z_lo, core).
Axes of the slice: x: 4, y: 4, z: 4 (z_hi: 2, z_lo: 2; z = z_hi * 2 + z_lo), core: 2. Of those that a mesh axis runs over, the one named last changes fastest.
Arguments:
- amps_ao: bfloat16 [1024, 65536], P('pair'), may hold values from -6 to 6
- integrals: bfloat16 [65536, 16384], P('pair', 'ao'), may hold values from -0.0234375 to 0.0234375
- tile_sizes: int32 [256], P('pair'), may hold values from 1 to 256, 39321 in all
- pair_list: int32 [1024, 2], P('pair'), may hold values from 0 to 199, as said below
- partner: int32 [1024], replicated, may hold values from 0 to 1023, as said below
- occ_energy: float32 [200], replicated, may hold values from -2 to -0.3
- vir_energy: float32 [128], replicated, may hold values from 0.2 to 3
- amplitudes: float32 [1024, 16384], P('pair', 'ao'), may hold values from -3 to 3
- other_terms: float32 [1024, 16384], P('pair', 'ao'), may hold values from -6 to 6
Outputs:
- residual: float32 [1024, 16384], P('pair', 'ao')
- updated: float32 [1024, 16384], P('pair', 'ao')
Inputs may be any that keep to these rules, and one draw needn't show every extreme that they name: `pair_list`: every pair i, j has i != j, appears once, and its pair j, i appears too. partner is an involution without fixed points, and pair_list[partner[p]] is pair_list[p] reversed. With B = 32, partner[p] // 32 equals (p // 32 + B // 2) mod B.
All inputs are finite; a program needn't handle non-finite values. No bound on the sum of `tile_sizes` on one device may be relied on, other than what follows from the above.
Results may differ from a plain program's by a relative error of at most 0.0003.
Values may be sent and summed in bfloat16 or wider, within the bound.
A program may use at most 192 MiB of HBM per device.

v0:
```python
import jax
import jax.numpy as jnp
from jax import lax
from jax.sharding import PartitionSpec as P

NOCC = 200
NL = 128
TILE = 256


def shifted(block, axis, distance):
    devices = range(lax.axis_size(axis))
    route = [((i - distance) % len(devices), i) for i in devices]
    return lax.ppermute(block, axis, route)


def local(
    amps_ao,
    integrals,
    tile_sizes,
    pair_list,
    partner,
    occ_energy,
    vir_energy,
    amplitudes,
    other_terms,
):
    slot_count = amps_ao.shape[0]
    col_count = integrals.shape[1]
    lam_rows = NL // lax.axis_size("ao")
    live_rows = jnp.arange(TILE)[None, :] < tile_sizes[:, None]
    screened = jnp.where(live_rows.reshape(-1, 1), integrals, jnp.zeros((), jnp.bfloat16))
    slices = lax.all_to_all(amps_ao, "pair", split_axis=1, concat_axis=0, tiled=True)
    own_first = lax.axis_index("pair") * slot_count
    lam_first = lax.axis_index("ao") * lam_rows
    own_partner = lax.dynamic_slice_in_dim(partner, own_first, slot_count, 0)
    ladder = lax.psum_scatter(
        jnp.dot(slices, screened, preferred_element_type=jnp.float32),
        "pair",
        scatter_dimension=0,
        tiled=True,
    )
    half_axis = lax.axis_size("pair") // 2
    neighbour = shifted(ladder, "pair", half_axis)
    source_first = (lax.axis_index("pair") + half_axis) % lax.axis_size("pair") * slot_count
    mirrored = neighbour[own_partner - source_first].reshape(slot_count, lam_rows, NL)
    arrived = lax.all_to_all(mirrored, "ao", split_axis=2, concat_axis=1, tiled=True)
    symmetric = 0.5 * (ladder + jnp.swapaxes(arrived, 1, 2).reshape(slot_count, col_count))
    occ_index = jnp.arange(NOCC, dtype=jnp.int32)
    picked = jnp.where(
        pair_list[:, :, None] == occ_index[None, None, :],
        occ_energy[None, None, :],
        jnp.float32(0.0),
    )
    occ_sum = jnp.sum(picked, axis=(1, 2))
    vir_rows = lax.dynamic_slice_in_dim(vir_energy, lam_first, lam_rows, 0)
    vir_pairs = (vir_rows[:, None] + vir_energy[None, :]).reshape(-1)
    denominator = vir_pairs[None, :] - occ_sum[:, None]
    residual = other_terms + symmetric - denominator * amplitudes
    updated = amplitudes + residual / denominator
    return (residual, updated)


def solution(mesh):
    in_specs = (
        P("pair", None),
        P("pair", "ao"),
        P("pair"),
        P("pair", None),
        P(),
        P(),
        P(),
        P("pair", "ao"),
        P("pair", "ao"),
    )
    out_specs = (P("pair", "ao"), P("pair", "ao"))
    return jax.shard_map(local, mesh=mesh, in_specs=in_specs, out_specs=out_specs, check_vma=False)
```

profile of v0, /device:TPU:1, one launch (start us, length us, event | category | flops | bytes accessed | tf_op | source)
XLA Modules:
  0.0 395.2 jit_solution(11469008048847000467)
XLA Ops:
  7.2 4.7 %copy.60 = bf16[4,32,8,2048]{3,2,0,1:T(8,128)(2,1)} copy(bf16[4,32,8,2048]{3,2,1,0:T(8,128)(2,1)} %bitcast.36) | data formatting | bytes 8388608 | tf_op jit(solution)/shard_map/all_to_all | solution.py:33
  11.9 11.4 %all-to-all-start = ((bf16[32,32,2048]{2,0,1:T(8,128)(2,1)}), bf16[32,32,2048]{2,0,1:T(8,128)(2,1)}, u32[]{:S(2)}, u32[]{:S(2)}) async-start(bf16[32,32,2048]{2,0,1:T(8,128)(2,1)} %bitcast.33), calls=%async_computation | async-start | bytes 8388608 | tf_op jit(solution)/shard_map/all_to_all | solution.py:33
  23.5 51.4 %all-to-all-done = bf16[32,32,2048]{2,0,1:T(8,128)(2,1)} async-done(((bf16[32,32,2048]{2,0,1:T(8,128)(2,1)}), bf16[32,32,2048]{2,0,1:T(8,128)(2,1)}, u32[]{:S(2)}, u32[]{:S(2)}) %all-to-all-start) | async-done | bytes 4194336 | tf_op jit(solution)/shard_map/all_to_all | solution.py:33
  74.9 25.5 %fusion.3 = f32[1024,4096]{0,1:T(8,128)} fusion(bf16[1024,2048]{1,0:T(8,128)(2,1)} %bitcast.1, bf16[2048,4096]{1,0:T(8,128)(2,1)} %param.10, pred[2048]{0:T(1024)(128)(4,1)S(1)} %lt.41), kind=kOutput, calls=%fused_computation.4 | convolution fusion | flops 17188257792 | bytes 37750784 | tf_op jit(solution)/shard_map/dot_general | solution.py:38
  100.4 17.5 %copy.55 = f32[1024,4096]{1,0:T(8,128)} copy(f32[1024,4096]{0,1:T(8,128)} %fusion.3) | data formatting | bytes 33554432
  117.9 207.0 %reduce-scatter.4.cloned.1.call-done = f32[32,4096]{1,0:T(8,128)} async-done(((f32[1024,4096]{1,0:T(8,128)}), f32[32,4096]{1,0:T(8,128)}) %reduce-scatter.4.cloned.1.call-update) | async-done | bytes 524304 | tf_op jit(solution)/shard_map/reduce_scatter | solution.py:37
  324.9 0.6 collective-permute-start
  325.5 0.8 compare_select_fusion
  326.3 13.0 %collective-permute-done = f32[32,4096]{1,0:T(8,128)S(1)} collective-permute-done((f32[32,4096]{1,0:T(8,128)}, f32[32,4096]{1,0:T(8,128)S(1)}, u32[]{:S(2)}, u32[]{:S(2)}) %collective-permute-start) | collective-permute-done | bytes 524320 | tf_op jit(solution)/shard_map/ppermute | solution.py:14
  339.2 0.7 gather_fusion
  340.1 1.8 copy.48
  341.9 1.6 reshape.61
  343.6 20.2 %all-to-all-start.1 = ((f32[4,1,32768]{2,1,0:T(1,128)}), f32[4,1,32768]{2,1,0:T(1,128)S(1)}, u32[]{:S(2)}, u32[]{:S(2)}) async-start(f32[4,1,32768]{2,1,0:T(1,128)} %reshape.61), calls=%async_computation.1 | async-start | bytes 1048576 | tf_op jit(solution)/shard_map/all_to_all | solution.py:47
  363.8 0.6 copy.50
  364.4 3.1 copy.51
  367.8 1.9 copy.56
  369.7 2.0 all-to-all-done.1
  371.7 0.5 broadcast.19
  372.2 2.1 reduce
  374.4 2.1 reshape.62
  376.4 2.9 copy.49
  379.4 4.5 %fusion.8 = (f32[32,4096]{0,1:T(8,128)}, f32[32,4096]{0,1:T(8,128)}) fusion(f32[32,4096]{0,1:T(8,128)} %copy.51, f32[32]{0:T(128)S(1)} %select_reduce_fusion, f32[4096]{0:T(1024)S(1)} %add_bitcast_fusion, f32[32,4096]{0,1:T(8,128)S(1)} %copy.50, f32[32,4096]{0,1:T(8,128)} %copy.56, f32[32,4,32,32]{0,2,1,3:T(8,128)} %copy.49), kind=kLoop, calls=%fused_computation.10 | loop fusion | flops 1048576 | bytes 3162240 | tf_op jit(solution)/shard_map/add | solution.py:60
  383.8 3.1 copy.53
  387.0 1.4 copy.54
  (23 shorter events, 0.6 us)
Async XLA Ops:
  11.9 11.5 %copy-start.5 = (s32[8]{0:T(128)S(1)}, s32[8]{0:T(128)}, u32[]{:S(2)}) copy-start(s32[8]{0:T(128)} %param.11) | copy-start | bytes 100
  11.9 63.0 %all-to-all-start = ((bf16[32,32,2048]{2,0,1:T(8,128)(2,1)}), bf16[32,32,2048]{2,0,1:T(8,128)(2,1)}, u32[]{:S(2)}, u32[]{:S(2)}) async-start(bf16[32,32,2048]{2,0,1:T(8,128)(2,1)} %bitcast.33), calls=%async_computation | async-start | bytes 8388608 | tf_op jit(solution)/shard_map/all_to_all | solution.py:33
  23.3 301.5 %reduce-scatter.4.cloned.1.call-start = ((), (), s32[]{:S(2)}) async-start(), calls=%async_computation.3 | async-start | bytes 17301504 | tf_op jit(solution)/shard_map/reduce_scatter | solution.py:37
  324.9 14.4 %collective-permute-start = (f32[32,4096]{1,0:T(8,128)}, f32[32,4096]{1,0:T(8,128)S(1)}, u32[]{:S(2)}, u32[]{:S(2)}) collective-permute-start(f32[32,4096]{1,0:T(8,128)} %reduce-scatter.4.cloned.1.call-done), channel_id=1, source_target_pairs={{64,0},{68,4},{72,8},{76,12},{80,16},{84,20},{88,24},{92,28},{96,3... | collective-permute-start | bytes 1572872 | tf_op jit(solution)/shard_map/ppermute | solution.py:14
  341.9 21.8 %copy-start.1 = (f32[32,4096]{1,0:T(8,128)S(1)}, f32[32,4096]{1,0:T(8,128)}, u32[]{:S(2)}) copy-start(f32[32,4096]{1,0:T(8,128)} %param.17) | copy-start | bytes 1572868
  343.6 28.1 %all-to-all-start.1 = ((f32[4,1,32768]{2,1,0:T(1,128)}), f32[4,1,32768]{2,1,0:T(1,128)S(1)}, u32[]{:S(2)}, u32[]{:S(2)}) async-start(f32[4,1,32768]{2,1,0:T(1,128)} %reshape.61), calls=%async_computation.1 | async-start | bytes 1048576 | tf_op jit(solution)/shard_map/all_to_all | solution.py:47
  363.7 3.7 copy-start.6
  363.7 3.8 copy-start.3
  363.7 3.8 copy-start.4
  364.4 3.4 copy-start.2
  383.8 3.1 copy-start
Sparse Core Ops, SparseCore 0:
  118.0 206.8 reduce-scatter.3
where the time goes:
time: 396 us; the launch traced here: 395 us
  waiting for transfers between devices  273 us (69%)
  local copies, waits for them, and re-layouts  42.2 us (11%)
  starting transfers between devices  32.3 us (8%)
  matrix products  25.5 us (6%)
  between operations  14.1 us (4%)
  other arithmetic  7.71 us (2%)
    reduce_scatter x1, waiting for transfers between devices, local(): lax.psum_scatter(jnp.dot(slices, screened, preferred_element_type=jnp.flo...  207 us
    all_to_all x1, waiting for transfers between devices, local(): lax.all_to_all(amps_ao, 'pair', split_axis=1, concat_axis=0, tiled=True)  51.4 us
    unnamed x23, local copies, waits for them, and re-layouts  31.4 us
    dot_general x1, matrix products, local(): jnp.dot(slices, screened, preferred_element_type=jnp.float32)  25.5 us
    all_to_all x1, starting transfers between devices, local(): lax.all_to_all(mirrored, 'ao', split_axis=2, concat_axis=1, tiled=True)  20.2 us
    ppermute x1, waiting for transfers between devices, shifted(): return lax.ppermute(block, axis, route)  13 us
    all_to_all x1, starting transfers between devices, local(): lax.all_to_all(amps_ao, 'pair', split_axis=1, concat_axis=0, tiled=True)  11.4 us
  transfers between devices with their start and end apart: 4, of which 4 were waited for; matrix products, arithmetic and copies ran while one was open for 2% of the time, Pallas kernels for 0%

commit v1 on v0

v1 whole, which is shorter than its diff:
```python
import functools

import jax
import jax.numpy as jnp
from jax import lax
from jax.experimental import pallas as pl
from jax.experimental.pallas import tpu as pltpu
from jax.sharding import PartitionSpec as P

NOCC = 200
NL = 128
TILE = 256
ROWS = 32
SLAB = 2048
HALF = SLAB // 2
COLS = 4096
C = 512
NK = COLS // 2 // C
MESH = pl.DeviceIdType.MESH

STEPS = 32760.0
LIMIT = (288.0, 1152.0, 4608.0)
FLOOR = (2.0**-12, 2.0**-11, 2.0**-10)
OCTAVES = (20.1699, 21.1699, 22.1699)


def encode(value, stage):
    level = jnp.log2(1.0 + jnp.abs(value) * (1.0 / FLOOR[stage])) * (STEPS / OCTAVES[stage])
    level = jnp.where(value < 0.0, -level, level)
    return jnp.round(level).astype(jnp.int32).astype(jnp.int16)


def decode(code, stage):
    level = code.astype(jnp.int32).astype(jnp.float32)
    size = (jnp.exp2(jnp.abs(level) * (OCTAVES[stage] / STEPS)) - 1.0) * FLOOR[stage]
    return jnp.where(level < 0.0, -size, size)


def ladder_kernel(
    amps, integrals, sizes, out,
    a, b, total, own1, out1, in1, out2, in2, out3, in3, mask,
    amp_send, amp_recv, mate_send, mate_recv, own_sem, b_sem,
    send1, recv1, send2, recv2, send3, recv3,
):
    pair, ao = lax.axis_index("pair"), lax.axis_index("ao")
    zh, y, x = pair // 16, (pair // 4) % 4, pair % 4
    zl, core = ao // 2, ao % 2
    mate = (pair, zl * 2 + 1 - core)
    across = (((zh + 1) % 2) * 16 + y * 4 + x, ao)

    def offset(j):
        return j // 16, (j // 4) % 4, j % 4

    def target(j):
        dz, dy, dx = offset(j)
        there = ((zh + dz) % 2) * 16 + ((y + dy) % 4) * 4 + (x + dx) % 4
        return there, ((zl + dz) % 2) * 2 + core

    def ring(part, j):
        if part == 0:
            return zh * 16 + y * 4 + (x + j) % 4, ao
        return zh * 16 + ((y + j) % 4) * 4 + x, ao

    barrier = pltpu.get_barrier_semaphore()

    def greet(j, carry):
        pl.semaphore_signal(barrier, inc=1, device_id=target(j), device_id_type=MESH)
        return carry

    lax.fori_loop(1, 32, greet, 0)
    for peer in (mate, across):
        pl.semaphore_signal(barrier, inc=1, device_id=peer, device_id_type=MESH)
    pl.semaphore_wait(barrier, 33)

    def rows_of(sx, sy, sz, half):
        return a.at[sx, sy, pl.ds(sz * ROWS, ROWS), pl.ds(half * HALF, HALF)]

    def amp_copy(j):
        there, their_ao = target(j)
        return pltpu.make_async_remote_copy(
            src_ref=amps.at[:, pl.ds(there * SLAB + core * HALF, HALF)],
            dst_ref=rows_of(x, y, zh, core),
            send_sem=amp_send.at[j - 1], recv_sem=amp_recv.at[j - 1],
            device_id=(there, their_ao), device_id_type=MESH)

    def arrived(j, half, send, recv):
        dz, dy, dx = offset(j)
        block = rows_of((x + 4 - dx) % 4, (y + 4 - dy) % 4, (zh + dz) % 2, half)
        return pltpu.make_async_remote_copy(
            src_ref=block, dst_ref=block, send_sem=send.at[j - 1], recv_sem=recv.at[j - 1],
            device_id=mate, device_id_type=MESH)

    def start_amp(j, carry):
        amp_copy(j).start()
        return carry

    lax.fori_loop(1, 32, start_amp, 0)
    own_copy = pltpu.make_async_copy(
        amps.at[:, pl.ds(pair * SLAB, SLAB)], a.at[x, y, pl.ds(zh * ROWS, ROWS), :], own_sem)
    own_copy.start()

    def b_copy(i):
        cols = pl.ds(i * C, C)
        return pltpu.make_async_copy(integrals.at[:, cols], b.at[:, cols], b_sem.at[i])

    for k in range(NK):
        b_copy(k).start()
        b_copy(NK + k).start()

    lane = lax.broadcasted_iota(jnp.int32, (16, TILE), 1)
    for t in range(SLAB // TILE):
        mask[:, t * TILE:(t + 1) * TILE] = jnp.where(lane < sizes[t], 1.0, 0.0).astype(jnp.bfloat16)

    def forward(j, carry):
        arrived(j, core, amp_send, amp_recv).wait_recv()
        arrived(j, core, mate_send, mate_recv).start()
        return carry

    lax.fori_loop(1, 32, forward, 0)

    def settle(j, carry):
        arrived(j, 1 - core, mate_send, mate_recv).wait_recv()
        arrived(j, core, mate_send, mate_recv).wait_send()
        amp_copy(j).wait_send()
        return carry

    lax.fori_loop(1, 32, settle, 0)
    own_copy.wait()

    def screen(i, carry):
        for r in range(4):
            rows = pl.ds(r * 16, 16)
            a[i // 4, i % 4, rows, :] = a[i // 4, i % 4, rows, :] * mask[...]
        return carry

    lax.fori_loop(0, 16, screen, 0)

    def copy1(part, k, j):
        return pltpu.make_async_remote_copy(
            src_ref=out1.at[part, k, j], dst_ref=in1.at[part, k, j],
            send_sem=send1.at[part, k, j], recv_sem=recv1.at[part, k, j],
            device_id=ring(part, j + 1), device_id_type=MESH)

    def copy2(part, k, j):
        return pltpu.make_async_remote_copy(
            src_ref=out2.at[part, k, j], dst_ref=in2.at[part, k, j],
            send_sem=send2.at[part, k, j], recv_sem=recv2.at[part, k, j],
            device_id=ring(1 - part, j + 1), device_id_type=MESH)

    def copy3(part, k):
        return pltpu.make_async_remote_copy(
            src_ref=out3.at[part, k], dst_ref=in3.at[part, k],
            send_sem=send3.at[part, k], recv_sem=recv3.at[part, k],
            device_id=across, device_id_type=MESH)

    def block_of(part, d):
        block = total[d] if part == 0 else total[:, d]
        return block.reshape(256, C)

    def multiply(k, carry):
        for part in range(2):
            i = part * NK + k
            b_copy(i).wait()
            total[...] = jnp.dot(
                a[...].reshape(1024, SLAB), b[:, pl.ds(pl.multiple_of(i * C, C), C)],
                preferred_element_type=jnp.float32).reshape(4, 4, 64, C)
            here = x if part == 0 else y

            def push(j, inner):
                out1[part, k, j] = encode(block_of(part, (here + j + 1) % 4), 0)
                copy1(part, k, j).start()
                return inner

            lax.fori_loop(0, 3, push, 0)
            own1[part, k] = block_of(part, here)
        return carry

    lax.fori_loop(0, NK, multiply, 0)

    def reduce1(k, carry):
        for part in range(2):
            for j in range(3):
                copy1(part, k, j).wait_recv()
            there = y if part == 0 else x

            def summed(d):
                rows = pl.ds(pl.multiple_of(d * 64, 64), 64)
                value = own1[part, k, rows, :]
                for j in range(3):
                    value = value + decode(in1[part, k, j, rows, :], 0)
                return value

            def push(j, inner):
                out2[part, k, j] = encode(summed((there + j + 1) % 4), 1)
                copy2(part, k, j).start()
                return inner

            lax.fori_loop(0, 3, push, 0)
            rows = pl.ds(pl.multiple_of(there * 64, 64), 64)
            own1[part, k, rows, :] = summed(there)
        return carry

    lax.fori_loop(0, NK, reduce1, 0)

    def reduce2(k, carry):
        for part in range(2):
            there = y if part == 0 else x
            rows = pl.ds(pl.multiple_of(there * 64, 64), 64)
            value = own1[part, k, rows, :]
            for j in range(3):
                copy2(part, k, j).wait_recv()
                value = value + decode(in2[part, k, j], 1)
            out3[part, k] = encode(value, 2)
            copy3(part, k).start()
            own1[part, k, rows, :] = value
        return carry

    lax.fori_loop(0, NK, reduce2, 0)

    def finish(k, carry):
        for part in range(2):
            there = y if part == 0 else x
            rows = pl.ds(pl.multiple_of(there * 64, 64), 64)
            copy3(part, k).wait_recv()
            cols = pl.ds(pl.multiple_of((part * NK + k) * C, C), C)
            out[:, cols] = own1[part, k, rows, :] + decode(in3[part, k], 2)
            copy3(part, k).wait_send()
            for j in range(3):
                copy1(part, k, j).wait_send()
                copy2(part, k, j).wait_send()
        return carry

    lax.fori_loop(0, NK, finish, 0)


def ladder_rows(amps_ao, integrals, tile_sizes):
    sem = pltpu.SemaphoreType.DMA
    vmem = pltpu.VMEM
    return pl.pallas_call(
        ladder_kernel,
        out_shape=jax.ShapeDtypeStruct((64, COLS), jnp.float32),
        in_specs=[
            pl.BlockSpec(memory_space=pl.ANY),
            pl.BlockSpec(memory_space=pl.ANY),
            pl.BlockSpec(memory_space=pltpu.SMEM),
        ],
        out_specs=pl.BlockSpec(memory_space=pltpu.VMEM),
        scratch_shapes=[
            vmem((4, 4, 64, SLAB), jnp.bfloat16),
            vmem((SLAB, COLS), jnp.bfloat16),
            vmem((4, 4, 64, C), jnp.float32),
            vmem((2, NK, 256, C), jnp.float32),
            vmem((2, NK, 3, 256, C), jnp.int16),
            vmem((2, NK, 3, 256, C), jnp.int16),
            vmem((2, NK, 3, 64, C), jnp.int16),
            vmem((2, NK, 3, 64, C), jnp.int16),
            vmem((2, NK, 64, C), jnp.int16),
            vmem((2, NK, 64, C), jnp.int16),
            vmem((16, SLAB), jnp.bfloat16),
            sem((31,)), sem((31,)), sem((31,)), sem((31,)), sem, sem((2 * NK,)),
            sem((2, NK, 3)), sem((2, NK, 3)), sem((2, NK, 3)), sem((2, NK, 3)),
            sem((2, NK)), sem((2, NK)),
        ],
        compiler_params=pltpu.CompilerParams(
            collective_id=0, has_side_effects=True, vmem_limit_bytes=60 << 20),
        cost_estimate=pl.CostEstimate(
            flops=2 * 1024 * SLAB * COLS, bytes_accessed=24 << 20, transcendentals=0),
        name="ladder",
    )(amps_ao, integrals, tile_sizes)


def local(
    amps_ao,
    integrals,
    tile_sizes,
    pair_list,
    partner,
    occ_energy,
    vir_energy,
    amplitudes,
    other_terms,
):
    slot_count = amps_ao.shape[0]
    col_count = integrals.shape[1]
    lam_rows = NL // lax.axis_size("ao")
    own_first = lax.axis_index("pair") * slot_count
    lam_first = lax.axis_index("ao") * lam_rows
    own_partner = lax.dynamic_slice_in_dim(partner, own_first, slot_count, 0)
    both = ladder_rows(amps_ao, integrals, tile_sizes)
    zh = lax.axis_index("pair") // 16
    ladder = lax.dynamic_slice_in_dim(both, zh * ROWS, ROWS, 0)
    neighbour = lax.dynamic_slice_in_dim(both, (1 - zh) * ROWS, ROWS, 0)
    mirrored = neighbour[own_partner % ROWS].reshape(slot_count, lam_rows, NL)
    arrived = lax.all_to_all(mirrored, "ao", split_axis=2, concat_axis=1, tiled=True)
    symmetric = 0.5 * (ladder + jnp.swapaxes(arrived, 1, 2).reshape(slot_count, col_count))
    occ_index = jnp.arange(NOCC, dtype=jnp.int32)
    picked = jnp.where(
        pair_list[:, :, None] == occ_index[None, None, :],
        occ_energy[None, None, :],
        jnp.float32(0.0),
    )
    occ_sum = jnp.sum(picked, axis=(1, 2))
    vir_rows = lax.dynamic_slice_in_dim(vir_energy, lam_first, lam_rows, 0)
    vir_pairs = (vir_rows[:, None] + vir_energy[None, :]).reshape(-1)
    denominator = vir_pairs[None, :] - occ_sum[:, None]
    residual = other_terms + symmetric - denominator * amplitudes
    updated = amplitudes + residual / denominator
    return (residual, updated)


def solution(mesh):
    in_specs = (
        P("pair", None),
        P("pair", "ao"),
        P("pair"),
        P("pair", None),
        P(),
        P(),
        P(),
        P("pair", "ao"),
        P("pair", "ao"),
    )
    out_specs = (P("pair", "ao"), P("pair", "ao"))
    return jax.shard_map(local, mesh=mesh, in_specs=in_specs, out_specs=out_specs, check_vma=False)
```

time: 396 us -> 146 us (0.37)
  waiting for transfers between devices: 273 us -> 7.25 us
  Pallas kernels: 0 us -> 116 us
  local copies, waits for them, and re-layouts: 42.2 us -> 12 us
  starting transfers between devices: 32.3 us -> 4.79 us
  matrix products: 25.5 us -> 0 us
  between operations: 14.1 us -> 0.77 us
    reduce_scatter x1 -> x0, waiting for transfers between devices: 207 us -> none  [local(): lax.psum_scatter(jnp.dot(slices, screened, preferred_element_type=jnp.flo...]
    pallas_call x0 -> x1, Pallas kernels: none -> 116 us  [ladder_rows(): pl.pallas_call(ladder_kernel, out_shape=jax.ShapeDtypeStruct((64, COLS),...]
    all_to_all x1 -> x0, waiting for transfers between devices: 51.4 us -> none  [local(): lax.all_to_all(amps_ao, 'pair', split_axis=1, concat_axis=0, tiled=True)]
    unnamed x23 -> x15, local copies, waits for them, and re-layouts: 31.4 us -> 2.48 us
    dot_general x1 -> x0, matrix products: 25.5 us -> none  [local(): jnp.dot(slices, screened, preferred_element_type=jnp.float32)]
    all_to_all x1, starting transfers between devices: 20.2 us -> 4.79 us  [local(): lax.all_to_all(mirrored, 'ao', split_axis=2, concat_axis=1, tiled=True)]
    ppermute x1 -> x0, waiting for transfers between devices: 13 us -> none  [shifted(): return lax.ppermute(block, axis, route)]
    all_to_all x1 -> x0, starting transfers between devices: 11.4 us -> none  [local(): lax.all_to_all(amps_ao, 'pair', split_axis=1, concat_axis=0, tiled=True)]
  transfers between devices with their start and end apart: 4 -> 1, of which waited for: 4 -> 1; matrix products, arithmetic and copies ran while one was open for 2% -> 0% of each run, Pallas kernels for 0% -> 0%
where the time goes in v1:
time: 146 us; the launch traced here: 145 us
  Pallas kernels  116 us (79%)
  local copies, waits for them, and re-layouts  12 us (8%)
  waiting for transfers between devices  7.25 us (5%)
  starting transfers between devices  4.79 us (3%)
  other arithmetic  4.56 us (3%)
    pallas_call x1, Pallas kernels, ladder_rows(): pl.pallas_call(ladder_kernel, out_shape=jax.ShapeDtypeStruct((64, COLS),...  116 us
    all_to_all x1, waiting for transfers between devices, local(): lax.all_to_all(mirrored, 'ao', split_axis=2, concat_axis=1, tiled=True)  7.25 us
    all_to_all x3, local copies, waits for them, and re-layouts, local(): lax.all_to_all(mirrored, 'ao', split_axis=2, concat_axis=1, tiled=True)  5.77 us
    all_to_all x1, starting transfers between devices, local(): lax.all_to_all(mirrored, 'ao', split_axis=2, concat_axis=1, tiled=True)  4.79 us
  transfers between devices with their start and end apart: 1, of which 1 were waited for; matrix products, arithmetic and copies ran while one was open for 0% of the time, Pallas kernels for 0%

profile of v1, /device:TPU:1, one launch (start us, length us, event | category | flops | bytes accessed | tf_op | source)
XLA Modules:
  0.0 145.3 jit_solution(4439352398202271611)
XLA Ops:
  0.7 0.8 compare_select_fusion
  1.4 116.0 %ladder.1 = f32[64,4096]{1,0:T(8,128)} custom-call(bf16[32,65536]{1,0:T(8,128)(2,1)} %amps.1, bf16[2048,4096]{1,0:T(8,128)(2,1)} %integrals.1, s32[8]{0:T(128)} %sizes.1), custom_call_target="tpu_custom_call" | custom-call | flops 17179869184 | bytes 25165824 | tf_op jit(solution)/shard_map/ladder/pallas_call | solution.py:239
  117.4 1.1 constant_dynamic-slice_fusion
  118.5 0.7 gather_fusion
  119.3 0.1 copy.18
  119.4 1.8 %copy.16 = f32[32,32,128]{1,0,2:T(8,128)S(1)} copy(f32[32,32,128]{2,1,0:T(8,128)S(1)} %bitcast.25) | data formatting | bytes 1048576 | tf_op jit(solution)/shard_map/reshape | solution.py:293
  121.2 0.0 copy-start.5
  121.2 0.0 copy-start.3
  121.2 0.0 copy-start.4
  121.2 1.6 %reshape.40 = f32[4,1,32768]{2,1,0:T(1,128)} reshape(f32[128,32,32]{2,1,0:T(8,128)S(1)} %bitcast.22) | data formatting | bytes 1048576
  122.9 4.8 %all-to-all-start = ((f32[4,1,32768]{2,1,0:T(1,128)}), f32[4,1,32768]{2,1,0:T(1,128)S(1)}, u32[]{:S(2)}, u32[]{:S(2)}) async-start(f32[4,1,32768]{2,1,0:T(1,128)} %reshape.40), calls=%async_computation | async-start | bytes 1048576 | tf_op jit(solution)/shard_map/all_to_all | solution.py:294
  127.7 0.0 copy-done.5
  127.7 0.1 dynamic_slice.15
  127.7 0.0 copy-done.3
  127.7 0.0 copy-done.4
  127.7 0.2 select_reduce_fusion
  127.9 0.1 add_bitcast_fusion
  128.0 7.3 %all-to-all-done = f32[4,1,32768]{2,1,0:T(1,128)S(1)} async-done(((f32[4,1,32768]{2,1,0:T(1,128)}), f32[4,1,32768]{2,1,0:T(1,128)S(1)}, u32[]{:S(2)}, u32[]{:S(2)}) %all-to-all-start) | async-done | bytes 524320 | tf_op jit(solution)/shard_map/all_to_all | solution.py:294
  135.3 0.5 broadcast.22
  135.8 2.1 %reduce = f32[4,32768]{1,0:T(4,128)S(1)} reduce(f32[4,1,32768]{2,1,0:T(1,128)S(1)} %all-to-all-done, f32[]{:T(128)} %broadcast.22), dimensions={1}, to_apply=%all_to_all.13.reduce_sub_computation | reduce | bytes 1048580 | tf_op jit(solution)/shard_map/all_to_all | solution.py:294
  137.9 0.7 reshape.41
  138.6 2.7 %copy.17 = f32[32,4,32,32]{2,1,3,0:T(4,128)} copy(f32[32,4,32,32]{2,0,3,1:T(8,128)S(1)} %bitcast.23) | data formatting | bytes 1048576 | tf_op jit(solution)/shard_map/all_to_all | solution.py:294
  141.3 2.6 %all_to_all.16 = f32[32,128,32]{1,2,0:T(8,128)S(1)} reshape(f32[32,4,32,32]{2,1,3,0:T(4,128)} %copy.17) | data formatting | bytes 1048576 | tf_op jit(solution)/shard_map/all_to_all | solution.py:294
  143.9 1.4 fusion.1
  (7 shorter events, 0.0 us)
Async XLA Ops:
  121.2 6.5 %copy-start.5 = (f32[128]{0:T(128)S(1)}, f32[128]{0:T(128)}, u32[]{:S(2)}) copy-start(f32[128]{0:T(128)} %param.15) | copy-start | bytes 1540
  121.2 6.5 %copy-start.3 = (f32[200]{0:T(256)S(1)}, f32[200]{0:T(256)}, u32[]{:S(2)}) copy-start(f32[200]{0:T(256)} %param.14) | copy-start | bytes 2404
  121.2 6.5 %copy-start.4 = (s32[32,2]{0,1:T(2,128)S(1)}, s32[32,2]{0,1:T(2,128)}, u32[]{:S(2)}) copy-start(s32[32,2]{0,1:T(2,128)} %param.12) | copy-start | bytes 772
  122.9 12.4 %all-to-all-start = ((f32[4,1,32768]{2,1,0:T(1,128)}), f32[4,1,32768]{2,1,0:T(1,128)S(1)}, u32[]{:S(2)}, u32[]{:S(2)}) async-start(f32[4,1,32768]{2,1,0:T(1,128)} %reshape.40), calls=%async_computation | async-start | bytes 1048576 | tf_op jit(solution)/shard_map/all_to_all | solution.py:294
  141.3 2.6 %copy-start = (f32[64,4096]{1,0:T(8,128)S(1)}, f32[64,4096]{1,0:T(8,128)}, u32[]{:S(2)}) copy-start(f32[64,4096]{1,0:T(8,128)} %ladder.1) | copy-start | bytes 3145732
  141.3 2.6 %copy-start.1 = (f32[32,4096]{1,0:T(8,128)S(1)}, f32[32,4096]{1,0:T(8,128)}, u32[]{:S(2)}) copy-start(f32[32,4096]{1,0:T(8,128)} %param.16) | copy-start | bytes 1572868
  141.3 2.6 %copy-start.2 = (f32[32,4096]{1,0:T(8,128)S(1)}, f32[32,4096]{1,0:T(8,128)}, u32[]{:S(2)}) copy-start(f32[32,4096]{1,0:T(8,128)} %param.17) | copy-start | bytes 1572868

commit v2 on v0

v2 whole, which is shorter than its diff:
```python
import functools

import jax
import jax.numpy as jnp
from jax import lax
from jax.experimental import pallas as pl
from jax.experimental.pallas import tpu as pltpu
from jax.sharding import PartitionSpec as P

NL = 128
TILE = 256
ROWS = 32
SLAB = 2048
HALF = SLAB // 2
QUARTER = SLAB // 4
COLS = 4096
LAMS = 32
C = 512
NK = COLS // 2 // C
MESH = pl.DeviceIdType.MESH

STEPS = 32760.0
LIMIT = (288.0, 1152.0, 4608.0)
FLOOR = (2.0**-12, 2.0**-11, 2.0**-10)
OCTAVES = (20.1699, 21.1699, 22.1699)


def encode(value, stage):
    level = jnp.log2(1.0 + jnp.abs(value) * (1.0 / FLOOR[stage])) * (STEPS / OCTAVES[stage])
    level = jnp.where(value < 0.0, -level, level)
    return jnp.round(level).astype(jnp.int32).astype(jnp.int16)


def decode(code, stage):
    level = code.astype(jnp.int32).astype(jnp.float32)
    size = (jnp.exp2(jnp.abs(level) * (OCTAVES[stage] / STEPS)) - 1.0) * FLOOR[stage]
    return jnp.where(level < 0.0, -size, size)


def ladder_kernel(
    amps, integrals, sizes, out, turned,
    a, b, staged, total, own1, out1, in1, out2, in2, out3, in3, mask, rows3, out4, in4,
    b_sem, own_sem, half_send, half_recv, mate_send, mate_recv, z_send, z_recv, plane_send, plane_recv,
    group_send, group_recv, send1, recv1, send2, recv2, send3, recv3, send4, recv4,
):
    pair, ao = lax.axis_index("pair"), lax.axis_index("ao")
    zh, y, x = pair // 16, (pair // 4) % 4, pair % 4
    zl, core = ao // 2, ao % 2
    mate = (pair, zl * 2 + 1 - core)
    beside = (pair, (1 - zl) * 2 + core)
    opposite = ((1 - zh) * 16 + y * 4 + x, (1 - zl) * 2 + core)
    across = ((1 - zh) * 16 + y * 4 + x, ao)

    def in_plane(i):
        return ((y + i // 4) % 4) * 4 + (x + i % 4) % 4

    def ring(part, j):
        if part == 0:
            return zh * 16 + y * 4 + (x + j) % 4, ao
        return zh * 16 + ((y + j) % 4) * 4 + x, ao

    def remote(src, dst, send, recv, device):
        return pltpu.make_async_remote_copy(
            src_ref=src, dst_ref=dst, send_sem=send, recv_sem=recv,
            device_id=device, device_id_type=MESH)

    def each(first, last, body):
        def step(i, carry):
            body(i)
            return carry

        lax.fori_loop(first, last, step, 0)

    barrier = pltpu.get_barrier_semaphore()

    def greet(peer):
        pl.semaphore_signal(barrier, inc=1, device_id=peer, device_id_type=MESH)

    each(1, 16, lambda i: greet((zh * 16 + in_plane(i), ao)))
    for peer in (opposite, across, *((pair, (ao + i) % 4) for i in range(1, 4))):
        greet(peer)
    pl.semaphore_wait(barrier, 20)

    def half_cols(half):
        return pl.ds(pl.multiple_of(half * HALF, HALF), HALF)

    def half_copy(i):
        there = in_plane(i)
        first = (zh * 16 + there) * SLAB + core * HALF
        return remote(
            amps.at[:, pl.ds(pl.multiple_of(first, HALF), HALF)], a.at[0, x, y, :, half_cols(core)],
            half_send.at[i - 1], half_recv.at[i - 1], (zh * 16 + there, ao))

    def half_block(i, half):
        return a.at[0, (x + 4 - i % 4) % 4, (y + 4 - i // 4) % 4, :, half_cols(half)]

    def mate_copy(i, half):
        block = half_block(i, half)
        return remote(block, block, mate_send.at[i - 1], mate_recv.at[i - 1], mate)

    def quarter_cols(quarter):
        return pl.ds(pl.multiple_of(quarter * QUARTER, QUARTER), QUARTER)

    def z_copy(i):
        first = ((1 - zh) * 16 + i) * SLAB + ((1 - zl) * 2 + core) * QUARTER
        return remote(
            amps.at[:, pl.ds(pl.multiple_of(first, QUARTER), QUARTER)], staged.at[i],
            z_send.at[i], z_recv.at[i], opposite)

    def plane_copy(i):
        there = in_plane(i)
        return remote(
            staged.at[there], a.at[1, x, y, :, quarter_cols(ao)],
            plane_send.at[i - 1], plane_recv.at[i - 1], (zh * 16 + there, ao))

    def group_copy(kind, g, quarter, device):
        block = a.at[1, g, :, :, quarter_cols(quarter)]
        return remote(block, block, group_send.at[kind, g], group_recv.at[kind, g], device)

    each(1, 16, lambda i: half_copy(i).start())
    each(0, 16, lambda i: z_copy(i).start())
    own_copy = pltpu.make_async_copy(
        amps.at[:, pl.ds(pl.multiple_of(pair * SLAB, SLAB), SLAB)], a.at[0, x, y], own_sem)
    own_copy.start()

    def b_copy(t):
        cols = pl.ds(t * C, C)
        return pltpu.make_async_copy(integrals.at[:, cols], b.at[:, cols], b_sem.at[t])

    for k in range(NK):
        b_copy(k).start()
        b_copy(NK + k).start()

    lane = lax.broadcasted_iota(jnp.int32, (16, TILE), 1)
    for t in range(SLAB // TILE):
        mask[:, t * TILE:(t + 1) * TILE] = jnp.where(lane < sizes[t], 1.0, 0.0).astype(jnp.bfloat16)

    def screen(h):
        def block(i):
            for r in range(ROWS // 16):
                rows = pl.ds(r * 16, 16)
                a[h, i // 4, i % 4, rows, :] = a[h, i // 4, i % 4, rows, :] * mask[...]

        each(0, 16, block)

    def forward_half(i):
        half_copy(i).wait_recv()
        mate_copy(i, core).start()

    def settle_half(i):
        mate_copy(i, 1 - core).wait_recv()
        mate_copy(i, core).wait_send()
        half_copy(i).wait_send()

    each(1, 16, forward_half)
    each(1, 16, settle_half)
    own_copy.wait()
    screen(0)

    def copy1(h, t, j):
        part = t // NK
        there = jnp.where(part == 0, ring(0, j + 1)[0], ring(1, j + 1)[0])
        return remote(
            out1.at[h, t, j], in1.at[h, t, j], send1.at[h, t, j], recv1.at[h, t, j], (there, ao))

    def copy2(h, t, j):
        part = t // NK
        there = jnp.where(part == 0, ring(1, j + 1)[0], ring(0, j + 1)[0])
        return remote(
            out2.at[h, t, j], in2.at[h, t, j], send2.at[h, t, j], recv2.at[h, t, j], (there, ao))

    def copy3(h, t):
        return remote(
            out3.at[h, t], in3.at[1 - h, t], send3.at[h, t], recv3.at[1 - h, t], across)

    def multiply(h, k):
        for part in range(2):
            t = part * NK + k
            if h == 0:
                b_copy(t).wait()
            total[...] = jnp.dot(
                a[h].reshape(16 * ROWS, SLAB), b[:, pl.ds(pl.multiple_of(t * C, C), C)],
                preferred_element_type=jnp.float32).reshape(4, 4, ROWS, C)
            here = x if part == 0 else y

            def block_of(d):
                block = total[d] if part == 0 else total[:, d]
                return block.reshape(4 * ROWS, C)

            def push(j):
                out1[h, t, j] = encode(block_of((here + j + 1) % 4), 0)
                copy1(h, t, j).start()

            each(0, 3, push)
            own1[h, t] = block_of(here)

    def mine(t):
        return jnp.where(t // NK == 0, y, x)

    def rows_at(d):
        return pl.ds(pl.multiple_of(d * ROWS, ROWS), ROWS)

    def reduce1(h, t):
        for j in range(3):
            copy1(h, t, j).wait_recv()

        def summed(d):
            value = own1[h, t, rows_at(d), :]
            for j in range(3):
                value = value + decode(in1[h, t, j, rows_at(d), :], 0)
            return value

        def push(j):
            out2[h, t, j] = encode(summed((mine(t) + j + 1) % 4), 1)
            copy2(h, t, j).start()

        each(0, 3, push)
        own1[h, t, rows_at(mine(t)), :] = summed(mine(t))

    def reduce2(h, t):
        value = own1[h, t, rows_at(mine(t)), :]
        for j in range(3):
            copy2(h, t, j).wait_recv()
            value = value + decode(in2[h, t, j], 1)
        out3[h, t] = encode(value, 2)
        copy3(h, t).start()
        own1[h, t, rows_at(mine(t)), :] = value

    def finish(t):
        copy3(1, t).wait_recv()
        cols = pl.ds(pl.multiple_of(t * C, C), C)
        out[:, cols] = own1[0, t, rows_at(mine(t)), :] + decode(in3[0, t], 2)
        copy3(0, t).wait_recv()
        value = own1[1, t, rows_at(mine(t)), :] + decode(in3[1, t], 2)
        for l in range(C // NL):
            rows3[pl.ds(t * (C // NL) + l, ROWS, stride=LAMS), :] = value[:, l * NL:(l + 1) * NL]

    def both(k, body):
        body(k)
        body(NK + k)

    multiply(0, 0)

    each(0, 16, lambda i: z_copy(i).wait_recv())
    each(1, 16, lambda i: plane_copy(i).start())
    here_copy = pltpu.make_async_copy(
        staged.at[y * 4 + x], a.at[1, x, y, :, quarter_cols(ao)], own_sem)
    here_copy.start()

    multiply(0, 1)

    here_copy.wait()
    each(1, 16, lambda i: plane_copy(i).wait_recv())

    def relay(g):
        group_copy(0, g, ao, beside).start()
        group_copy(1, g, ao, mate).start()

    each(0, 4, relay)
    each(2, NK, lambda k: multiply(0, k))

    def relay_on(g):
        group_copy(0, g, (1 - zl) * 2 + core, beside).wait_recv()
        group_copy(2, g, (1 - zl) * 2 + core, mate).start()

    each(0, 4, relay_on)

    def settle(g):
        group_copy(1, g, zl * 2 + 1 - core, mate).wait_recv()
        group_copy(2, g, (1 - zl) * 2 + 1 - core, mate).wait_recv()
        group_copy(0, g, ao, beside).wait_send()
        group_copy(1, g, ao, mate).wait_send()
        group_copy(2, g, (1 - zl) * 2 + core, mate).wait_send()

    each(0, 4, settle)
    screen(1)

    def second(k):
        multiply(1, k)
        both(k, lambda t: reduce1(0, t))

    each(0, NK, second)

    def third(k):
        both(k, lambda t: reduce2(0, t))
        both(k, lambda t: reduce1(1, t))

    each(0, NK, third)
    each(0, NK, lambda k: both(k, lambda t: reduce2(1, t)))
    each(0, NK, lambda k: both(k, finish))

    def turn(q):
        block = rows3[pl.ds(pl.multiple_of(q * NL, NL), NL), :].T
        for d in range(4):
            out4[d, q] = block[d * LAMS:(d + 1) * LAMS]

    each(0, ROWS // 4, turn)

    def copy4(i):
        to = (ao + i) % 4
        return remote(out4.at[to], in4.at[3 - i], send4.at[i - 1], recv4.at[i - 1], (pair, to))

    for i in range(1, 4):
        copy4(i).start()
    turned[ao] = out4[ao]

    each(0, 16, lambda i: z_copy(i).wait_send())
    each(1, 16, lambda i: plane_copy(i).wait_send())

    def drain(t):
        for h in range(2):
            copy3(h, t).wait_send()
            for j in range(3):
                copy1(h, t, j).wait_send()
                copy2(h, t, j).wait_send()

    each(0, 2 * NK, drain)
    for i in range(1, 4):
        copy4(i).wait()
        turned[(ao + 4 - i) % 4] = in4[3 - i]


def ladder_rows(amps_ao, integrals, tile_sizes):
    sem = pltpu.SemaphoreType.DMA
    vmem = pltpu.VMEM
    tiles = 2 * NK
    return pl.pallas_call(
        ladder_kernel,
        out_shape=(
            jax.ShapeDtypeStruct((ROWS, COLS), jnp.float32),
            jax.ShapeDtypeStruct((4, ROWS // 4, LAMS, NL), jnp.float32),
        ),
        in_specs=[
            pl.BlockSpec(memory_space=pl.ANY),
            pl.BlockSpec(memory_space=pl.ANY),
            pl.BlockSpec(memory_space=pltpu.SMEM),
        ],
        out_specs=(pl.BlockSpec(memory_space=pltpu.VMEM), pl.BlockSpec(memory_space=pltpu.VMEM)),
        scratch_shapes=[
            vmem((2, 4, 4, ROWS, SLAB), jnp.bfloat16),
            vmem((SLAB, COLS), jnp.bfloat16),
            vmem((16, ROWS, QUARTER), jnp.bfloat16),
            vmem((4, 4, ROWS, C), jnp.float32),
            vmem((2, tiles, 4 * ROWS, C), jnp.float32),
            vmem((2, tiles, 3, 4 * ROWS, C), jnp.int16),
            vmem((2, tiles, 3, 4 * ROWS, C), jnp.int16),
            vmem((2, tiles, 3, ROWS, C), jnp.int16),
            vmem((2, tiles, 3, ROWS, C), jnp.int16),
            vmem((2, tiles, ROWS, C), jnp.int16),
            vmem((2, tiles, ROWS, C), jnp.int16),
            vmem((16, SLAB), jnp.bfloat16),
            vmem((ROWS * LAMS, NL), jnp.float32),
            vmem((4, ROWS // 4, LAMS, NL), jnp.float32),
            vmem((3, ROWS // 4, LAMS, NL), jnp.float32),
            sem((tiles,)), sem, sem((15,)), sem((15,)), sem((15,)), sem((15,)),
            sem((16,)), sem((16,)), sem((15,)), sem((15,)), sem((3, 4)), sem((3, 4)),
            sem((2, tiles, 3)), sem((2, tiles, 3)), sem((2, tiles, 3)), sem((2, tiles, 3)),
            sem((2, tiles)), sem((2, tiles)), sem((3,)), sem((3,)),
        ],
        compiler_params=pltpu.CompilerParams(
            collective_id=0, has_side_effects=True, vmem_limit_bytes=60 << 20),
        cost_estimate=pl.CostEstimate(
            flops=2 * 1024 * SLAB * COLS, bytes_accessed=24 << 20, transcendentals=0),
        name="ladder",
    )(amps_ao, integrals, tile_sizes)


def update_kernel(
    own, turned, partner, pairs, occ, vir, vir_row, amplitudes, other, residual, updated, swapped
):
    lam_first = lax.axis_index("ao") * LAMS
    lane = lax.broadcasted_iota(jnp.int32, (LAMS, NL), 1) // LAMS

    first = lax.axis_index("pair") * ROWS

    def assemble(s, carry):
        slot = lax.rem(partner[first + s], ROWS)
        q, j = lax.div(slot, 4), lax.rem(slot, 4)
        value = jnp.zeros((LAMS, NL), jnp.float32)
        for d in range(4):
            moved = pltpu.roll(turned[d, q], lax.rem(d + 4 - j, 4) * LAMS, 1)
            value = jnp.where(lane == d, moved, value)
        swapped[pl.ds(pl.multiple_of(s * LAMS, LAMS), LAMS), :] = value
        return carry

    lax.fori_loop(0, ROWS, assemble, 0, unroll=4)
    row = lax.broadcasted_iota(jnp.int32, (ROWS, NL), 0)
    occ_sum = jnp.zeros((ROWS, NL), jnp.float32)
    for s in range(ROWS):
        occ_sum = jnp.where(row == s, occ[pairs[s, 0]] + occ[pairs[s, 1]], occ_sum)
    sig = jnp.broadcast_to(vir_row[...].reshape(1, NL), (ROWS, NL))

    def finish(lam, carry):
        cols = pl.ds(pl.multiple_of(lam * NL, NL), NL)
        symmetric = 0.5 * (own[:, cols] + swapped[pl.ds(lam, ROWS, stride=LAMS), :])
        denominator = (vir[lam_first + lam] + sig) - occ_sum
        amps = amplitudes[:, cols]
        value = other[:, cols] + symmetric - denominator * amps
        residual[:, cols] = value
        updated[:, cols] = amps + value / denominator
        return carry

    lax.fori_loop(0, LAMS, finish, 0)


def update(own, turned, partner, pair_list, occ_energy, vir_energy, amplitudes, other_terms):
    smem, vmem = pl.BlockSpec(memory_space=pltpu.SMEM), pl.BlockSpec(memory_space=pltpu.VMEM)
    shape = jax.ShapeDtypeStruct((ROWS, COLS), jnp.float32)
    return pl.pallas_call(
        update_kernel,
        out_shape=(shape, shape),
        in_specs=[vmem, vmem, smem, smem, smem, smem, vmem, vmem, vmem],
        out_specs=(vmem, vmem),
        scratch_shapes=[pltpu.VMEM((ROWS * LAMS, NL), jnp.float32)],
        compiler_params=pltpu.CompilerParams(vmem_limit_bytes=32 << 20),
        cost_estimate=pl.CostEstimate(
            flops=8 * ROWS * COLS, bytes_accessed=3 << 20, transcendentals=0),
        name="update",
    )(own, turned, partner, pair_list, occ_energy, vir_energy, vir_energy, amplitudes, other_terms)


def local(
    amps_ao,
    integrals,
    tile_sizes,
    pair_list,
    partner,
    occ_energy,
    vir_energy,
    amplitudes,
    other_terms,
):
    own, turned = ladder_rows(amps_ao, integrals, tile_sizes)
    return update(own, turned, partner, pair_list, occ_energy, vir_energy, amplitudes, other_terms)


def solution(mesh):
    in_specs = (
        P("pair", None),
        P("pair", "ao"),
        P("pair"),
        P("pair", None),
        P(),
        P(),
        P(),
        P("pair", "ao"),
        P("pair", "ao"),
    )
    out_specs = (P("pair", "ao"), P("pair", "ao"))
    return jax.shard_map(local, mesh=mesh, in_specs=in_specs, out_specs=out_specs, check_vma=False)
```

time: 396 us -> 121 us (0.31)
  waiting for transfers between devices: 273 us -> 0 us
  Pallas kernels: 0 us -> 118 us
  local copies, waits for them, and re-layouts: 42.2 us -> 2.86 us
  starting transfers between devices: 32.3 us -> 0 us
  matrix products: 25.5 us -> 0 us
  between operations: 14.1 us -> 0.71 us
  other arithmetic: 7.71 us -> 0 us
    reduce_scatter x1 -> x0, waiting for transfers between devices: 207 us -> none  [local(): lax.psum_scatter(jnp.dot(slices, screened, preferred_element_type=jnp.flo...]
    pallas_call x0 -> x2, Pallas kernels: none -> 118 us  [the longest x1 114 us: ladder_rows(): pl.pallas_call(ladder_kernel, out_shape=(jax.ShapeDtypeStruct((ROWS, COLS...]
    all_to_all x2 -> x0, waiting for transfers between devices: 53.4 us -> none  [the longest x1 51.4 us: local(): lax.all_to_all(amps_ao, 'pair', split_axis=1, concat_axis=0, tiled=True)]
    all_to_all x2 -> x0, starting transfers between devices: 31.6 us -> none  [the longest x1 20.2 us: local(): lax.all_to_all(mirrored, 'ao', split_axis=2, concat_axis=1, tiled=True)]
    unnamed x23 -> x15, local copies, waits for them, and re-layouts: 31.4 us -> 2.86 us
    dot_general x1 -> x0, matrix products: 25.5 us -> none  [local(): jnp.dot(slices, screened, preferred_element_type=jnp.float32)]
    ppermute x1 -> x0, waiting for transfers between devices: 13 us -> none  [shifted(): return lax.ppermute(block, axis, route)]
    all_to_all x3 -> x0, local copies, waits for them, and re-layouts: 8.15 us -> none  [the longest x1 4.72 us: local(): lax.all_to_all(amps_ao, 'pair', split_axis=1, concat_axis=0, tiled=True)]
  transfers between devices with their start and end apart: 4 -> 0, of which waited for: 4 -> 0; matrix products, arithmetic and copies ran while one was open for 2% -> 0% of each run, Pallas kernels for 0% -> 0%
where the time goes in v2:
time: 121 us
  Pallas kernels  118 us (98%)
  local copies, waits for them, and re-layouts  2.86 us (2%)
    pallas_call x1, Pallas kernels, ladder_rows(): pl.pallas_call(ladder_kernel, out_shape=(jax.ShapeDtypeStruct((ROWS, COLS...  114 us
    pallas_call x1, Pallas kernels, update(): pl.pallas_call(update_kernel, out_shape=(shape, shape), in_specs=[vmem, v...  3.97 us
    unnamed x15, local copies, waits for them, and re-layouts  2.86 us

profile of v2, /device:TPU:1, one launch (start us, length us, event | category | flops | bytes accessed | tf_op | source)
XLA Modules:
  0.0 121.2 jit_solution(9815271088508751084)
XLA Ops:
  0.6 0.8 copy.11.pairs
  1.4 0.0 copy-start
  1.4 0.0 copy-start.1
  1.4 0.0 copy-start.4
  1.4 0.0 copy-start.5
  1.4 0.0 copy-start.6
  1.4 113.7 %ladder.1 = (f32[32,4096]{1,0:T(8,128)}, f32[4,8,32,128]{3,2,1,0:T(8,128)}) custom-call(bf16[32,65536]{1,0:T(8,128)(2,1)} %amps.1, bf16[2048,4096]{1,0:T(8,128)(2,1)} %integrals.1, s32[8]{0:T(128)} %sizes.1), custom_call_target="tpu_custom_call" | custom-call | flops 17179869184 | bytes 25165824 | tf_op jit(solution)/shard_map/ladder/pallas_call | solution.py:327
  115.1 0.0 copy-done
  115.1 0.0 copy-done.1
  115.1 0.0 copy-done.4
  115.1 0.0 copy-done.5
  115.2 0.0 copy-done.6
  115.2 0.0 copy-start.2
  115.2 1.0 copy-done.2
  116.2 0.0 copy-start.3
  116.2 1.0 copy-done.3
  117.2 4.0 %update.1 = (f32[32,4096]{1,0:T(8,128)}, f32[32,4096]{1,0:T(8,128)}) custom-call(f32[32,4096]{1,0:T(8,128)S(1)} %copy-done.2, f32[4,8,32,128]{3,2,1,0:T(8,128)S(1)} %copy-done.3, s32[1024]{0:T(1024)S(1)} %copy-done.4, s32[32,2]{1,0:T(8,128)S(1)} %copy.11.pairs, f32[200]{0:T(256)S(1)} %copy-done.6, f32[128]{0:T(128)S(1)} %copy-done.5, f32[128]{0:T(128)S(1)} %copy-done.5, ...), custom_call_target="tpu_custom_call" | custom-call | flops 1048576 | bytes 3145728 | tf_op jit(solution)/shard_map/update/pallas_call | solution.py:409
Async XLA Ops:
  1.4 113.7 %copy-start = (f32[32,4096]{1,0:T(8,128)S(1)}, f32[32,4096]{1,0:T(8,128)}, u32[]{:S(2)}) copy-start(f32[32,4096]{1,0:T(8,128)} %amplitudes.1) | copy-start | bytes 1572868
  1.4 113.7 %copy-start.1 = (f32[32,4096]{1,0:T(8,128)S(1)}, f32[32,4096]{1,0:T(8,128)}, u32[]{:S(2)}) copy-start(f32[32,4096]{1,0:T(8,128)} %other.1) | copy-start | bytes 1572868
  1.4 113.7 %copy-start.4 = (s32[1024]{0:T(1024)S(1)}, s32[1024]{0:T(1024)}, u32[]{:S(2)}) copy-start(s32[1024]{0:T(1024)} %partner.1) | copy-start | bytes 12292
  1.4 113.7 %copy-start.5 = (f32[128]{0:T(128)S(1)}, f32[128]{0:T(128)}, u32[]{:S(2)}) copy-start(f32[128]{0:T(128)} %vir_row.1) | copy-start | bytes 1540
  1.4 113.7 %copy-start.6 = (f32[200]{0:T(256)S(1)}, f32[200]{0:T(256)}, u32[]{:S(2)}) copy-start(f32[200]{0:T(256)} %occ.1) | copy-start | bytes 2404
  115.2 1.0 copy-start.2
  116.2 1.0 copy-start.3

commit v3 on v2

v3 whole, which is shorter than its diff:
```python
import functools

import jax
import jax.numpy as jnp
from jax import lax
from jax.experimental import pallas as pl
from jax.experimental.pallas import tpu as pltpu
from jax.sharding import PartitionSpec as P

NL = 128
TILE = 256
ROWS = 32
SLAB = 2048
QUARTER = SLAB // 4
COLS = 4096
LAMS = 32
C = 512
NK = COLS // 2 // C
LAGS = (1, 3, 5, 6)
MESH = pl.DeviceIdType.MESH

STEPS = 32760.0
OCTAVES = 20.17
FLOOR = 2.0**-12


def encode(value, slabs, twice=False):
    scale = jnp.where(twice, 0.5 / (FLOOR * slabs), 1.0 / (FLOOR * slabs))
    level = jnp.log2(1.0 + jnp.abs(value) * scale) * (STEPS / OCTAVES)
    level = jnp.where(value < 0.0, -level, level)
    return jnp.round(level).astype(jnp.int32).astype(jnp.int16)


def decode(code, slabs, twice=False):
    floor = jnp.where(twice, 2.0 * FLOOR * slabs, FLOOR * slabs)
    level = code.astype(jnp.int32).astype(jnp.float32)
    size = jnp.exp2(jnp.abs(level) * (OCTAVES / STEPS)) * floor - floor
    return jnp.where(level < 0.0, -size, size)


def ladder_kernel(
    amps, integrals, sizes, out, turned,
    a, b, staged, total, own1, keep, outz, inz, outo, ino, out1, in1, out2, in2, out3, in3, mask, rows3, out4, in4,
    b_sem, own_sem, here_sem, z_send, z_recv, plane_send, plane_recv, group_send, group_recv,
    sendz, recvz, sendo, recvo, send1, recv1, send2, recv2, send3, recv3, send4, recv4,
):
    pair, ao = lax.axis_index("pair"), lax.axis_index("ao")
    zh, y, x = pair // 16, (pair // 4) % 4, pair % 4
    zl, core = ao // 2, ao % 2
    mate = (pair, zl * 2 + 1 - core)
    beside = (pair, (1 - zl) * 2 + core)
    opposite = ((1 - zh) * 16 + y * 4 + x, (1 - zl) * 2 + core)
    across = ((1 - zh) * 16 + y * 4 + x, ao)

    def in_plane(i):
        return ((y + i // 4) % 4) * 4 + (x + i % 4) % 4

    def ring(part, j):
        if part == 0:
            return zh * 16 + y * 4 + (x + j) % 4, ao
        return zh * 16 + ((y + j) % 4) * 4 + x, ao

    def remote(src, dst, send, recv, device):
        return pltpu.make_async_remote_copy(
            src_ref=src, dst_ref=dst, send_sem=send, recv_sem=recv,
            device_id=device, device_id_type=MESH)

    def sent(ref, sem):
        remote(ref, ref, sem, sem, mate).wait_send()

    def received(ref, sem):
        remote(ref, ref, sem, sem, mate).wait_recv()

    def each(first, last, body):
        def step(i, carry):
            body(i)
            return carry

        lax.fori_loop(first, last, step, 0)

    barrier = pltpu.get_barrier_semaphore()

    def greet(peer):
        pl.semaphore_signal(barrier, inc=1, device_id=peer, device_id_type=MESH)

    each(1, 16, lambda i: greet((zh * 16 + in_plane(i), ao)))
    for peer in (opposite, across, *((pair, (ao + i) % 4) for i in range(1, 4))):
        greet(peer)
    pl.semaphore_wait(barrier, 20)

    def quarter_cols(quarter):
        return pl.ds(pl.multiple_of(quarter * QUARTER, QUARTER), QUARTER)

    def amp_cols(position, quarter):
        return amps.at[:, pl.ds(pl.multiple_of(position * SLAB + quarter * QUARTER, QUARTER), QUARTER)]

    def z_copy(i):
        return remote(
            amp_cols((1 - zh) * 16 + i, (1 - zl) * 2 + core), staged.at[i],
            z_send, z_recv, opposite)

    def plane_copy(h, i):
        there = in_plane(i)
        return remote(
            amp_cols(zh * 16 + there, ao) if h == 0 else staged.at[there],
            a.at[h, x, y, :, quarter_cols(ao)],
            plane_send.at[h], plane_recv.at[h, i % 4], (zh * 16 + there, ao))

    def group_copy(h, kind, g, quarter, device):
        block = a.at[h, (x + 4 - g) % 4, :, :, quarter_cols(quarter)]
        recv = group_recv.at[h, g if kind == 0 else 3 + kind]
        return remote(block, block, group_send.at[h], recv, device)

    def relay(h, g):
        column = a.at[h, (x + 4 - g) % 4, :, :, quarter_cols(ao)]
        received(column if g else column.at[pl.ds(0, 3)], plane_recv.at[h, g])
        group_copy(h, 0, g, ao, beside).start()
        group_copy(h, 1, g, ao, mate).start()

    def relay_on(h, g):
        group_copy(h, 0, g, (1 - zl) * 2 + core, beside).wait_recv()
        group_copy(h, 2, g, (1 - zl) * 2 + core, mate).start()

    def settle(h):
        whole = a.at[h, :, :, :, quarter_cols(0)]
        received(whole, group_recv.at[h, 4])
        received(whole, group_recv.at[h, 5])
        sent(a.at[h, :, :, :, pl.ds(0, 3 * QUARTER)], group_send.at[h])

    each(1, 16, lambda i: plane_copy(0, (i % 4) * 4 + i // 4).start())
    each(0, 16, lambda i: z_copy(i).start())
    own_copy = pltpu.make_async_copy(
        amp_cols(pair, ao), a.at[0, x, y, :, quarter_cols(ao)], own_sem)
    own_copy.start()

    def b_copy(t):
        cols = pl.ds(t * C, C)
        return pltpu.make_async_copy(integrals.at[:, cols], b.at[:, cols], b_sem.at[t])

    for k in range(NK):
        b_copy(k).start()
        b_copy(NK + k).start()

    lane = lax.broadcasted_iota(jnp.int32, (16, TILE), 1)
    for t in range(SLAB // TILE):
        mask[:, t * TILE:(t + 1) * TILE] = jnp.where(lane < sizes[t], 1.0, 0.0).astype(jnp.bfloat16)

    def screen(h):
        def block(i):
            for r in range(ROWS // 16):
                rows = pl.ds(r * 16, 16)
                a[h, i // 4, i % 4, rows, :] = a[h, i // 4, i % 4, rows, :] * mask[...]

        each(0, 16, block)

    own_copy.wait()
    for g in range(4):
        relay(0, g)
    for g in range(4):
        relay_on(0, g)
    received(staged, z_recv)
    each(1, 16, lambda i: plane_copy(1, (i % 4) * 4 + i // 4).start())
    here_copy = pltpu.make_async_copy(
        staged.at[y * 4 + x], a.at[1, x, y, :, quarter_cols(ao)], here_sem)
    here_copy.start()
    settle(0)
    screen(0)

    def neighbour(t, side):
        along_x, along_y = ring(0, 1 + 2 * side)[0], ring(1, 1 + 2 * side)[0]
        return jnp.where(t // NK == 0, along_x, along_y), ao

    LAST = NK - 1

    def slot(h, t):
        return jnp.where(h == 0, t // NK * LAST + t % NK, 2 * LAST + t)

    def pair_slot(h, k):
        return jnp.where(h == 0, k, LAST + k)

    def copyo(s, t, side):
        return remote(
            outo.at[s, side], ino.at[s, side], sendo, recvo.at[s], neighbour(t, side))

    def copy1(s, t, side):
        return remote(
            out1.at[s, side], in1.at[s, side], send1, recv1.at[s], neighbour(t, side))

    def copy2(s, t, j):
        part = t // NK
        there = jnp.where(part == 0, ring(1, j + 1)[0], ring(0, j + 1)[0])
        return remote(out2.at[s, j], in2.at[s, j], send2, recv2.at[s], (there, ao))

    def copy3(h, k):
        to = (1 - h) * NK + k
        return remote(out3.at[pair_slot(h, k)], in3.at[to], send3, recv3.at[to], across)

    def copyz(part):
        return remote(outz.at[part], inz.at[part], sendz, recvz.at[part], across)

    def multiply(n):
        h, k = n // NK, n % NK
        for part in range(2):
            t = part * NK + k

            @pl.when(h == 0)
            def _():
                b_copy(t).wait()

            total[...] = jnp.dot(
                a[h].reshape(16 * ROWS, SLAB), b[:, pl.ds(pl.multiple_of(t * C, C), C)],
                preferred_element_type=jnp.float32).reshape(4, 4, ROWS, C)
            here = x if part == 0 else y

            @pl.when(n == LAST)
            def _():
                def block(d):
                    outz[part, d] = encode(total[d], 1)

                each(0, 4, block)
                copyz(part).start()

            @pl.when(n == NK + LAST)
            def _():
                copyz(part).wait_recv()

                def block(d):
                    total[d] = total[d] + decode(inz[part, d], 1)

                each(0, 4, block)

            def block_of(d):
                block = total[d] if part == 0 else total[:, d]
                return block.reshape(4 * ROWS, C)

            @pl.when(n != LAST)
            def _():
                across_block = block_of((here + 2) % 4)
                s = slot(h, t)
                for side in range(2):
                    outo[s, side] = encode(
                        across_block[:, side * C // 2:(side + 1) * C // 2], 1, k == LAST)
                    copyo(s, t, side).start()
                for side in range(2):
                    keep[t, side] = block_of((here + 1 + 2 * side) % 4)
                own1[h, t] = block_of(here)

    def combine(h, t):
        s, twice = slot(h, t), t % NK == LAST
        received(ino.at[s], recvo.at[s])
        for side in range(2):
            half = slice(side * C // 2, (side + 1) * C // 2)
            rest = slice((1 - side) * C // 2, (2 - side) * C // 2)
            out1[s, side, :, half] = encode(
                keep[t, side, :, half] + decode(ino[s, side], 1, twice), 2, twice)
            out1[s, side, :, rest] = encode(keep[t, side, :, rest], 2, twice)
            copy1(s, t, side).start()

    def mine(t):
        return jnp.where(t // NK == 0, y, x)

    def rows_at(d):
        return pl.ds(pl.multiple_of(d * ROWS, ROWS), ROWS)

    def reduce1(h, t):
        s, twice = slot(h, t), t % NK == LAST
        received(in1.at[s], recv1.at[s])

        def summed(d):
            value = own1[h, t, rows_at(d), :]
            for side in range(2):
                value = value + decode(in1[s, side, rows_at(d), :], 2, twice)
            return value

        def push(j):
            out2[s, j] = encode(summed((mine(t) + j + 1) % 4), 4, twice)
            copy2(s, t, j).start()

        each(0, 3, push)
        own1[h, t, rows_at(mine(t)), :] = summed(mine(t))

    def reduce2(h, k):
        twice = k == LAST
        for part in range(2):
            t = part * NK + k
            s = slot(h, t)
            received(in2.at[s], recv2.at[s])
            value = own1[h, t, rows_at(mine(t)), :]
            for j in range(3):
                value = value + decode(in2[s, j], 4, twice)
            out3[pair_slot(h, k), part] = encode(value, 16, twice)
            own1[h, t, rows_at(mine(t)), :] = value
        copy3(h, k).start()

    def finish(k, last):
        received(in3.at[k], recv3.at[k])
        if not last:
            received(in3.at[NK + k], recv3.at[NK + k])
        for part in range(2):
            t = part * NK + k
            cols = pl.ds(pl.multiple_of(t * C, C), C)
            value = own1[1, t, rows_at(mine(t)), :]
            if last:
                out[:, cols] = decode(in3[k, part], 32)
            else:
                out[:, cols] = own1[0, t, rows_at(mine(t)), :] + decode(in3[k, part], 16)
                value = value + decode(in3[NK + k, part], 16)
            for l in range(C // NL):
                rows3[pl.ds(t * (C // NL) + l, ROWS, stride=LAMS), :] = (
                    value[:, l * NL:(l + 1) * NL])

    def both(k, body):
        body(k)
        body(NK + k)

    def step(n):
        def at(lag, body):
            @pl.when((n >= lag) & (n < lag + 2 * NK) & (n != lag + LAST))
            def _():
                body((n - lag) // NK, (n - lag) % NK)

        def tiles_at(lag, body):
            at(lag, lambda h, k: both(k, lambda t: body(h, t)))

        @pl.when((n < 2 * NK) & (n != NK))
        def _():
            multiply(n)

        @pl.when(n == 0)
        def _():
            here_copy.wait()
            for g in range(4):
                relay(1, g)

        tiles_at(LAGS[0], combine)
        tiles_at(LAGS[1], reduce1)
        at(LAGS[2], reduce2)

        @pl.when((n >= NK + LAGS[3]) & (n < NK + LAGS[3] + LAST))
        def _():
            finish(n - NK - LAGS[3], False)

        @pl.when(n == NK)
        def _():
            for g in range(4):
                relay_on(1, g)
            settle(1)
            screen(1)
            multiply(n)

    each(0, NK + max(LAGS[3] + LAST, LAGS[2] + NK), step)
    finish(LAST, True)

    def turn(q):
        block = rows3[pl.ds(pl.multiple_of(q * NL, NL), NL), :].T
        for d in range(4):
            out4[d, q] = encode(block[d * LAMS:(d + 1) * LAMS], 32)

    each(0, ROWS // 4, turn)

    def copy4(i):
        to = (ao + i) % 4
        return remote(out4.at[to], in4.at[3 - i], send4, recv4, (pair, to))

    for i in range(1, 4):
        copy4(i).start()
    turned[ao] = out4[ao]

    sent(staged, z_send)
    for h in range(2):
        sent(staged.at[pl.ds(0, 15)], plane_send.at[h])
    for ref, sem in (
        (outo, sendo), (out1, send1), (out2, send2), (out3, send3), (outz, sendz),
        (out4.at[pl.ds(0, 3)], send4),
    ):
        sent(ref, sem)
    received(in4, recv4)
    for i in range(1, 4):
        turned[(ao + 4 - i) % 4] = in4[3 - i]


def ladder_rows(amps_ao, integrals, tile_sizes):
    sem = pltpu.SemaphoreType.DMA
    vmem = pltpu.VMEM
    tiles, slots = 2 * NK, 4 * NK - 2
    return pl.pallas_call(
        ladder_kernel,
        out_shape=(
            jax.ShapeDtypeStruct((ROWS, COLS), jnp.float32),
            jax.ShapeDtypeStruct((4, ROWS // 4, LAMS, NL), jnp.int16),
        ),
        in_specs=[
            pl.BlockSpec(memory_space=pl.ANY),
            pl.BlockSpec(memory_space=pl.ANY),
            pl.BlockSpec(memory_space=pltpu.SMEM),
        ],
        out_specs=(pl.BlockSpec(memory_space=pltpu.VMEM), pl.BlockSpec(memory_space=pltpu.VMEM)),
        scratch_shapes=[
            vmem((2, 4, 4, ROWS, SLAB), jnp.bfloat16),
            vmem((SLAB, COLS), jnp.bfloat16),
            vmem((16, ROWS, QUARTER), jnp.bfloat16),
            vmem((4, 4, ROWS, C), jnp.float32),
            vmem((2, tiles, 4 * ROWS, C), jnp.float32),
            vmem((tiles, 2, 4 * ROWS, C), jnp.float32),
            vmem((2, 4, 4, ROWS, C), jnp.int16),
            vmem((2, 4, 4, ROWS, C), jnp.int16),
            vmem((slots, 2, 4 * ROWS, C // 2), jnp.int16),
            vmem((slots, 2, 4 * ROWS, C // 2), jnp.int16),
            vmem((slots, 2, 4 * ROWS, C), jnp.int16),
            vmem((slots, 2, 4 * ROWS, C), jnp.int16),
            vmem((slots, 3, ROWS, C), jnp.int16),
            vmem((slots, 3, ROWS, C), jnp.int16),
            vmem((slots // 2, 2, ROWS, C), jnp.int16),
            vmem((tiles, 2, ROWS, C), jnp.int16),
            vmem((16, SLAB), jnp.bfloat16),
            vmem((ROWS * LAMS, NL), jnp.float32),
            vmem((4, ROWS // 4, LAMS, NL), jnp.int16),
            vmem((3, ROWS // 4, LAMS, NL), jnp.int16),
            sem((tiles,)), sem, sem, sem, sem, sem((2,)), sem((2, 4)), sem((2,)), sem((2, 6)),
            sem, sem((2,)), sem, sem((slots,)), sem, sem((slots,)), sem, sem((slots,)),
            sem, sem((tiles,)), sem, sem,
        ],
        compiler_params=pltpu.CompilerParams(
            collective_id=0, has_side_effects=True, vmem_limit_bytes=60 << 20),
        cost_estimate=pl.CostEstimate(
            flops=2 * 1024 * SLAB * COLS, bytes_accessed=24 << 20, transcendentals=0),
        name="ladder",
    )(amps_ao, integrals, tile_sizes)


def update_kernel(
    own_hbm, turned_hbm, partner, pairs, occ, vir, vir_row, amplitudes_hbm, other_hbm,
    residual, updated, swapped, own, turned, amplitudes, other, sem
):
    turned_copy = pltpu.make_async_copy(turned_hbm, turned, sem.at[0])
    row_copies = [
        pltpu.make_async_copy(src, dst, sem.at[i + 1])
        for i, (src, dst) in enumerate(
            ((own_hbm, own), (amplitudes_hbm, amplitudes), (other_hbm, other)))]
    turned_copy.start()
    for copy in row_copies:
        copy.start()
    lam_first = lax.axis_index("ao") * LAMS
    lane = lax.broadcasted_iota(jnp.int32, (LAMS, NL), 1) // LAMS

    row = lax.broadcasted_iota(jnp.int32, (ROWS, NL), 0)
    occ_sum = jnp.zeros((ROWS, NL), jnp.float32)
    for s in range(ROWS):
        occ_sum = jnp.where(row == s, occ[pairs[0, s]] + occ[pairs[1, s]], occ_sum)
    sig = jnp.broadcast_to(vir_row[...].reshape(1, NL), (ROWS, NL))

    turned_copy.wait()
    first = lax.axis_index("pair") * ROWS

    def assemble(s, carry):
        slot = lax.rem(partner[first + s], ROWS)
        q, j = lax.div(slot, 4), lax.rem(slot, 4)
        value = jnp.zeros((LAMS, NL), jnp.float32)
        for d in range(4):
            moved = pltpu.roll(decode(turned[d, q], 32), lax.rem(d + 4 - j, 4) * LAMS, 1)
            value = jnp.where(lane == d, moved, value)
        swapped[pl.ds(pl.multiple_of(s * LAMS, LAMS), LAMS), :] = value
        return carry

    lax.fori_loop(0, ROWS, assemble, 0, unroll=4)
    for copy in row_copies:
        copy.wait()

    def finish(lam, carry):
        cols = pl.ds(pl.multiple_of(lam * NL, NL), NL)
        symmetric = 0.5 * (own[:, cols] + swapped[pl.ds(lam, ROWS, stride=LAMS), :])
        denominator = (vir[lam_first + lam] + sig) - occ_sum
        amps = amplitudes[:, cols]
        value = other[:, cols] + symmetric - denominator * amps
        residual[:, cols] = value
        updated[:, cols] = amps + value / denominator
        return carry

    lax.fori_loop(0, LAMS, finish, 0)


def update(own, turned, partner, pair_list, occ_energy, vir_energy, amplitudes, other_terms):
    hbm = pl.BlockSpec(memory_space=pl.ANY)
    smem, vmem = pl.BlockSpec(memory_space=pltpu.SMEM), pl.BlockSpec(memory_space=pltpu.VMEM)
    shape = jax.ShapeDtypeStruct((ROWS, COLS), jnp.float32)
    return pl.pallas_call(
        update_kernel,
        out_shape=(shape, shape),
        in_specs=[hbm, hbm, smem, smem, smem, smem, vmem, hbm, hbm],
        out_specs=(vmem, vmem),
        scratch_shapes=[
            pltpu.VMEM((ROWS * LAMS, NL), jnp.float32),
            pltpu.VMEM((ROWS, COLS), jnp.float32),
            pltpu.VMEM((4, ROWS // 4, LAMS, NL), jnp.int16),
            pltpu.VMEM((ROWS, COLS), jnp.float32),
            pltpu.VMEM((ROWS, COLS), jnp.float32),
            pltpu.SemaphoreType.DMA((4,)),
        ],
        compiler_params=pltpu.CompilerParams(vmem_limit_bytes=60 << 20),
        cost_estimate=pl.CostEstimate(
            flops=8 * ROWS * COLS, bytes_accessed=3 << 20, transcendentals=0),
        name="update",
    )(own, turned, partner, pair_list.T, occ_energy, vir_energy, vir_energy, amplitudes, other_terms)


def local(
    amps_ao,
    integrals,
    tile_sizes,
    pair_list,
    partner,
    occ_energy,
    vir_energy,
    amplitudes,
    other_terms,
):
    own, turned = ladder_rows(amps_ao, integrals, tile_sizes)
    return update(own, turned, partner, pair_list, occ_energy, vir_energy, amplitudes, other_terms)


def solution(mesh):
    in_specs = (
        P("pair", None),
        P("pair", "ao"),
        P("pair"),
        P("pair", None),
        P(),
        P(),
        P(),
        P("pair", "ao"),
        P("pair", "ao"),
    )
    out_specs = (P("pair", "ao"), P("pair", "ao"))
    return jax.shard_map(local, mesh=mesh, in_specs=in_specs, out_specs=out_specs, check_vma=False)
```

time: 121 us -> 104 us (0.86)
  Pallas kernels: 118 us -> 103 us
  local copies, waits for them, and re-layouts: 2.86 us -> 0 us
    pallas_call x1, Pallas kernels: 114 us -> 97.7 us  [ladder_rows(): pl.pallas_call(ladder_kernel, out_shape=(jax.ShapeDtypeStruct((ROWS, COLS...]
    unnamed x15 -> x0, local copies, waits for them, and re-layouts: 2.86 us -> none
where the time goes in v3:
time: 104 us; the launch traced here: 103 us
  Pallas kernels  103 us (99%)
    pallas_call x1, Pallas kernels, ladder_rows(): pl.pallas_call(ladder_kernel, out_shape=(jax.ShapeDtypeStruct((ROWS, COLS...  97.7 us
    pallas_call x1, Pallas kernels, update(): pl.pallas_call(update_kernel, out_shape=(shape, shape), in_specs=[hbm, hb...  5 us

profile of v3, /device:TPU:1, one launch (start us, length us, event | category | flops | bytes accessed | tf_op | source)
XLA Modules:
  0.0 103.3 jit_solution(8325473450700193946)
XLA Ops:
  0.6 97.7 %ladder.1 = (f32[32,4096]{1,0:T(8,128)}, s16[4,8,32,128]{3,2,1,0:T(8,128)(2,1)}) custom-call(bf16[32,65536]{1,0:T(8,128)(2,1)} %amps.1, bf16[2048,4096]{1,0:T(8,128)(2,1)} %integrals.1, s32[8]{0:T(128)} %sizes.1), custom_call_target="tpu_custom_call" | custom-call | flops 17179869184 | bytes 25165824 | tf_op jit(solution)/shard_map/ladder/pallas_call | solution.py:386
  98.3 5.0 %update.1 = (f32[32,4096]{1,0:T(8,128)}, f32[32,4096]{1,0:T(8,128)}) custom-call(f32[32,4096]{1,0:T(8,128)} %get-tuple-element.4.own_hbm, s16[4,8,32,128]{3,2,1,0:T(8,128)(2,1)} %get-tuple-element.5.turned_hbm, s32[1024]{0:T(1024)} %partner.1, s32[2,32]{1,0:T(2,128)} %bitcast.1, f32[200]{0:T(256)} %occ.1, f32[128]{0:T(128)} %vir_row.1, f32[128]{0:T(128)} %vir_row.1, ...), custom_call_target="tpu_custom_call" | custom-call | flops 1048576 | bytes 3145728 | tf_op jit(solution)/shard_map/update/pallas_call | solution.py:486

commit v4 on v3

--- a/solution.py
+++ b/solution.py
@@ -40,7 +40,7 @@
 
 def ladder_kernel(
     amps, integrals, sizes, out, turned,
-    a, b, staged, total, own1, keep, outz, inz, outo, ino, out1, in1, out2, in2, out3, in3, mask, rows3, out4, in4,
+    a, b, staged, near, total, own1, keep, outz, inz, outo, ino, out1, in1, out2, in2, out3, in3, mask, rows3, out4, in4,
     b_sem, own_sem, here_sem, z_send, z_recv, plane_send, plane_recv, group_send, group_recv,
     sendz, recvz, sendo, recvo, send1, recv1, send2, recv2, send3, recv3, send4, recv4,
 ):
@@ -114,6 +114,12 @@
     def relay(h, g):
         column = a.at[h, (x + 4 - g) % 4, :, :, quarter_cols(ao)]
         received(column if g else column.at[pl.ds(0, 3)], plane_recv.at[h, g])
+
+        def screen(i):
+            rows = pl.ds(pl.multiple_of(i % 2 * 16, 16), 16)
+            column[i // 2, rows, :] = column[i // 2, rows, :] * mask[:, quarter_cols(ao)]
+
+        each(0, 2 * 4, screen)
         group_copy(h, 0, g, ao, beside).start()
         group_copy(h, 1, g, ao, mate).start()
 
@@ -121,11 +127,8 @@
         group_copy(h, 0, g, (1 - zl) * 2 + core, beside).wait_recv()
         group_copy(h, 2, g, (1 - zl) * 2 + core, mate).start()
 
-    def settle(h):
-        whole = a.at[h, :, :, :, quarter_cols(0)]
-        received(whole, group_recv.at[h, 4])
-        received(whole, group_recv.at[h, 5])
-        sent(a.at[h, :, :, :, pl.ds(0, 3 * QUARTER)], group_send.at[h])
+    def relayed(h, kind):
+        received(a.at[h, :, :, :, quarter_cols(0)], group_recv.at[h, 3 + kind])
 
     each(1, 16, lambda i: plane_copy(0, (i % 4) * 4 + i // 4).start())
     each(0, 16, lambda i: z_copy(i).start())
@@ -145,26 +148,35 @@
     for t in range(SLAB // TILE):
         mask[:, t * TILE:(t + 1) * TILE] = jnp.where(lane < sizes[t], 1.0, 0.0).astype(jnp.bfloat16)
 
-    def screen(h):
-        def block(i):
-            for r in range(ROWS // 16):
-                rows = pl.ds(r * 16, 16)
-                a[h, i // 4, i % 4, rows, :] = a[h, i // 4, i % 4, rows, :] * mask[...]
-
-        each(0, 16, block)
-
     own_copy.wait()
     for g in range(4):
         relay(0, g)
-    for g in range(4):
-        relay_on(0, g)
+    relayed(0, 1)
+
+    def k_half(side):
+        return pl.ds(pl.multiple_of(side * SLAB // 2, SLAB // 2), SLAB // 2)
+
+    def half_product(h, t, side):
+        return jnp.dot(
+            a[h, :, :, :, k_half(side)].reshape(16 * ROWS, SLAB // 2),
+            b[k_half(side), pl.ds(pl.multiple_of(t * C, C), C)],
+            preferred_element_type=jnp.float32)
+
+    def early(h, g):
+        for t in (g, NK + g):
+            if h == 0:
+                b_copy(t).wait()
+            near[t] = half_product(h, t, zl)
+        relay_on(h, g)
+
+    each(0, NK - 1, lambda g: early(0, g))
     received(staged, z_recv)
     each(1, 16, lambda i: plane_copy(1, (i % 4) * 4 + i // 4).start())
     here_copy = pltpu.make_async_copy(
         staged.at[y * 4 + x], a.at[1, x, y, :, quarter_cols(ao)], here_sem)
     here_copy.start()
-    settle(0)
-    screen(0)
+    early(0, NK - 1)
+    relayed(0, 2)
 
     def neighbour(t, side):
         along_x, along_y = ring(0, 1 + 2 * side)[0], ring(1, 1 + 2 * side)[0]
@@ -203,13 +215,7 @@
         for part in range(2):
             t = part * NK + k
 
-            @pl.when(h == 0)
-            def _():
-                b_copy(t).wait()
-
-            total[...] = jnp.dot(
-                a[h].reshape(16 * ROWS, SLAB), b[:, pl.ds(pl.multiple_of(t * C, C), C)],
-                preferred_element_type=jnp.float32).reshape(4, 4, ROWS, C)
+            total[...] = (near[t] + half_product(h, t, 1 - zl)).reshape(4, 4, ROWS, C)
             here = x if part == 0 else y
 
             @pl.when(n == LAST)
@@ -342,10 +348,9 @@
 
         @pl.when(n == NK)
         def _():
-            for g in range(4):
-                relay_on(1, g)
-            settle(1)
-            screen(1)
+            relayed(1, 1)
+            each(0, NK, lambda g: early(1, g))
+            relayed(1, 2)
             multiply(n)
 
     each(0, NK + max(LAGS[3] + LAST, LAGS[2] + NK), step)
@@ -369,6 +374,7 @@
     sent(staged, z_send)
     for h in range(2):
         sent(staged.at[pl.ds(0, 15)], plane_send.at[h])
+        sent(a.at[h, :, :, :, pl.ds(0, 3 * QUARTER)], group_send.at[h])
     for ref, sem in (
         (outo, sendo), (out1, send1), (out2, send2), (out3, send3), (outz, sendz),
         (out4.at[pl.ds(0, 3)], send4),
@@ -399,6 +405,7 @@
             vmem((2, 4, 4, ROWS, SLAB), jnp.bfloat16),
             vmem((SLAB, COLS), jnp.bfloat16),
             vmem((16, ROWS, QUARTER), jnp.bfloat16),
+            vmem((tiles, 16 * ROWS, C), jnp.float32),
             vmem((4, 4, ROWS, C), jnp.float32),
             vmem((2, tiles, 4 * ROWS, C), jnp.float32),
             vmem((tiles, 2, 4 * ROWS, C), jnp.float32),

time: 104 us -> 103 us (level)
  Pallas kernels: 103 us -> 101 us
    pallas_call x1, Pallas kernels: 97.7 us -> 96.1 us  [ladder_rows(): pl.pallas_call(ladder_kernel, out_shape=(jax.ShapeDtypeStruct((ROWS, COLS...]
where the time goes in v4:
time: 103 us; the launch traced here: 102 us
  Pallas kernels  101 us (98%)
    pallas_call x1, Pallas kernels, ladder_rows(): pl.pallas_call(ladder_kernel, out_shape=(jax.ShapeDtypeStruct((ROWS, COLS...  96.1 us
    pallas_call x1, Pallas kernels, update(): pl.pallas_call(update_kernel, out_shape=(shape, shape), in_specs=[hbm, hb...  5 us

profile of v4, /device:TPU:1, one launch (start us, length us, event | category | flops | bytes accessed | tf_op | source)
XLA Modules:
  0.0 101.7 jit_solution(90222855909110994)
XLA Ops:
  0.6 96.1 %ladder.1 = (f32[32,4096]{1,0:T(8,128)}, s16[4,8,32,128]{3,2,1,0:T(8,128)(2,1)}) custom-call(bf16[32,65536]{1,0:T(8,128)(2,1)} %amps.1, bf16[2048,4096]{1,0:T(8,128)(2,1)} %integrals.1, s32[8]{0:T(128)} %sizes.1), custom_call_target="tpu_custom_call" | custom-call | flops 17179869184 | bytes 25165824 | tf_op jit(solution)/shard_map/ladder/pallas_call | solution.py:392
  96.7 5.0 %update.1 = (f32[32,4096]{1,0:T(8,128)}, f32[32,4096]{1,0:T(8,128)}) custom-call(f32[32,4096]{1,0:T(8,128)} %get-tuple-element.4.own_hbm, s16[4,8,32,128]{3,2,1,0:T(8,128)(2,1)} %get-tuple-element.5.turned_hbm, s32[1024]{0:T(1024)} %partner.1, s32[2,32]{1,0:T(2,128)} %bitcast.1, f32[200]{0:T(256)} %occ.1, f32[128]{0:T(128)} %vir_row.1, f32[128]{0:T(128)} %vir_row.1, ...), custom_call_target="tpu_custom_call" | custom-call | flops 1048576 | bytes 3145728 | tf_op jit(solution)/shard_map/update/pallas_call | solution.py:493

commit v5 on v4

--- a/solution.py
+++ b/solution.py
@@ -420,7 +420,7 @@
             vmem((slots // 2, 2, ROWS, C), jnp.int16),
             vmem((tiles, 2, ROWS, C), jnp.int16),
             vmem((16, SLAB), jnp.bfloat16),
-            vmem((ROWS * LAMS, NL), jnp.float32),
+            vmem((ROWS * LAMS + LAMS, NL), jnp.float32),
             vmem((4, ROWS // 4, LAMS, NL), jnp.int16),
             vmem((3, ROWS // 4, LAMS, NL), jnp.int16),
             sem((tiles,)), sem, sem, sem, sem, sem((2,)), sem((2, 4)), sem((2,)), sem((2, 6)),
@@ -496,7 +496,7 @@
         in_specs=[hbm, hbm, smem, smem, smem, smem, vmem, hbm, hbm],
         out_specs=(vmem, vmem),
         scratch_shapes=[
-            pltpu.VMEM((ROWS * LAMS, NL), jnp.float32),
+            pltpu.VMEM((ROWS * LAMS + LAMS, NL), jnp.float32),
             pltpu.VMEM((ROWS, COLS), jnp.float32),
             pltpu.VMEM((4, ROWS // 4, LAMS, NL), jnp.int16),
             pltpu.VMEM((ROWS, COLS), jnp.float32),

time: 103 us -> 103 us (level)
  no operation moved by 1% of the time
where the time goes in v5:
time: 103 us; the launch traced here: 102 us
  Pallas kernels  101 us (98%)
    pallas_call x1, Pallas kernels, ladder_rows(): pl.pallas_call(ladder_kernel, out_shape=(jax.ShapeDtypeStruct((ROWS, COLS...  96.1 us
    pallas_call x1, Pallas kernels, update(): pl.pallas_call(update_kernel, out_shape=(shape, shape), in_specs=[hbm, hb...  5 us

profile of v5, /device:TPU:1, one launch (start us, length us, event | category | flops | bytes accessed | tf_op | source)
XLA Modules:
  0.0 101.7 jit_solution(8779048048145764899)
XLA Ops:
  0.6 96.1 %ladder.1 = (f32[32,4096]{1,0:T(8,128)}, s16[4,8,32,128]{3,2,1,0:T(8,128)(2,1)}) custom-call(bf16[32,65536]{1,0:T(8,128)(2,1)} %amps.1, bf16[2048,4096]{1,0:T(8,128)(2,1)} %integrals.1, s32[8]{0:T(128)} %sizes.1), custom_call_target="tpu_custom_call" | custom-call | flops 17179869184 | bytes 25165824 | tf_op jit(solution)/shard_map/ladder/pallas_call | solution.py:392
  96.7 5.0 %update.1 = (f32[32,4096]{1,0:T(8,128)}, f32[32,4096]{1,0:T(8,128)}) custom-call(f32[32,4096]{1,0:T(8,128)} %get-tuple-element.4.own_hbm, s16[4,8,32,128]{3,2,1,0:T(8,128)(2,1)} %get-tuple-element.5.turned_hbm, s32[1024]{0:T(1024)} %partner.1, s32[2,32]{1,0:T(2,128)} %bitcast.1, f32[200]{0:T(256)} %occ.1, f32[128]{0:T(128)} %vir_row.1, f32[128]{0:T(128)} %vir_row.1, ...), custom_call_target="tpu_custom_call" | custom-call | flops 1048576 | bytes 3145728 | tf_op jit(solution)/shard_map/update/pallas_call | solution.py:493
